TPU v7x, 32 devices: a whole 2x2x4 slice. The times are simulated.
32 devices in a mesh: row: 4 (over y, x), col: 8 (over z, core).
Axes of the slice: x: 2, y: 2, z: 4, core: 2. Of those that a mesh axis runs over, the one named last changes fastest.
Arguments:
- teacher_feats: bfloat16 [64, 64, 2048], P(None, 'row', 'col'), may hold values from -6 to 6
- teacher_probs: float32 [8, 64, 2048], P(None, 'row', 'col'), may hold values from 0 to 1, as said below
- student_feats: bfloat16 [256, 64, 2048], P(None, 'row', 'col'), may hold values from 0 to 8
- conv_weight: bfloat16 [9, 256, 256], replicated, may hold values from -0.125 to 0.125
- class_weight: bfloat16 [256, 8], replicated, may hold values from -3 to 3
Outputs:
- refined: float32 [8, 64, 2048], P(None, 'row', 'col')
- feature_grad: bfloat16 [256, 64, 2048], P(None, 'row', 'col')
- grad_conv: float32 [9, 256, 256], replicated
- grad_class: float32 [256, 8], replicated
Inputs may be any that keep to these rules, and one draw needn't show every extreme that they name: `teacher_probs`: at every pixel the 8 values are positive and sum to one.
All inputs are finite; a program needn't handle non-finite values.
Results may differ from a plain program's by a relative error of at most 0.002.
The roundings to bfloat16 on the way count: a program that leaves them out, or rounds other values in their place, can miss the bound.
Values may be sent and summed in bfloat16 or wider, within the bound.
A program may use at most 128 MiB of HBM per device.

v0:
```python
import functools

import jax
import jax.numpy as jnp
from jax import lax
from jax.experimental import pallas as pl
from jax.experimental.pallas import tpu as pltpu
from jax.sharding import PartitionSpec as P

ITERS = 4
REACH = 4
SHIFTS = (0, 1, 2, 4, -1, -2, -4)
SIDES = ((-1, 0), (1, 0), (0, -1), (0, 1), (-1, -1), (-1, 1), (1, -1), (1, 1))


def tap_list():
    offsets = []
    for radius in (1, 2, 4):
        for step_y in (-1, 0, 1):
            for step_x in (-1, 0, 1):
                if step_y != 0 or step_x != 0:
                    offsets.append((step_y * radius, step_x * radius))
    return offsets


MESH = pl.DeviceIdType.MESH


def remote(src, dst, sems, slot, row, col):
    return pltpu.make_async_remote_copy(
        src_ref=src,
        dst_ref=dst,
        send_sem=sems.at[0, slot],
        recv_sem=sems.at[1, slot],
        device_id=(row, col),
        device_id_type=MESH,
    )


def finish(copies):
    for copy in copies:
        copy.wait()


def reduce_body(nr, nz, scale, g_ref, cls_ref, out_ref, outc_ref, core_buf, row_buf, z_buf, fin, cls_core, cls_row, cls_z, sems):
    row = lax.axis_index("row")
    col = lax.axis_index("col")
    core = lax.rem(col, 2)
    z = col // 2
    twin = z * 2 + 1 - core
    total = g_ref.shape[0]
    part = total // nr
    piece = part // nz
    mine = pl.ds(pl.multiple_of(core * 128, 128), 128)
    other = pl.ds(pl.multiple_of((1 - core) * 128, 128), 128)
    slot = 0
    copies = [
        remote(g_ref.at[:, other], core_buf, sems, 0, row, twin),
        remote(cls_ref, cls_core, sems, 1, row, twin),
    ]
    for copy in copies:
        copy.start()
    yield
    finish(copies)
    slot = 2
    core_buf[...] = core_buf[...] + g_ref[:, mine]
    cls_row[row] = cls_ref[...] + cls_core[...]
    copies = []
    for step in range(1, nr):
        to = lax.rem(row + step, nr)
        copies.append(
            remote(core_buf.at[pl.ds(pl.multiple_of(to * part, 16), part)], row_buf.at[step - 1], sems, slot, to, col)
        )
        copies.append(remote(cls_row.at[row], cls_row.at[row], sems, slot + 1, to, col))
        slot += 2
    for copy in copies:
        copy.start()
    yield
    finish(copies)
    kept = pl.ds(pl.multiple_of(row * part, 16), part)
    summed = core_buf[kept]
    for step in range(1, nr):
        summed = summed + row_buf[step - 1]
    row_buf[0] = summed
    across = cls_row[0]
    for i in range(1, nr):
        across = across + cls_row[i]
    cls_z[z] = across
    copies = []
    for step in range(1, nz):
        to = lax.rem(z + step, nz)
        copies.append(
            remote(row_buf.at[0, pl.ds(pl.multiple_of(to * piece, 16), piece)], z_buf.at[step - 1], sems, slot, row, to * 2 + core)
        )
        copies.append(remote(cls_z.at[z], cls_z.at[z], sems, slot + 1, row, to * 2 + core))
        slot += 2
    for copy in copies:
        copy.start()
    yield
    finish(copies)
    summed = row_buf[0, pl.ds(pl.multiple_of(z * piece, 16), piece)]
    for step in range(1, nz):
        summed = summed + z_buf[step - 1]
    own = pl.ds(pl.multiple_of(row * part + z * piece, 16), piece)
    fin[core, own] = (summed * scale).astype(jnp.bfloat16)
    across = cls_z[0]
    for i in range(1, nz):
        across = across + cls_z[i]
    outc_ref[...] = across * scale
    copies = []
    for step in range(1, nz):
        to = lax.rem(z + step, nz)
        copies.append(remote(fin.at[core, own], fin.at[core, own], sems, slot, row, to * 2 + core))
        slot += 1
    for copy in copies:
        copy.start()
    yield
    finish(copies)
    copies = []
    for step in range(1, nr):
        to = lax.rem(row + step, nr)
        copies.append(remote(fin.at[core, kept], fin.at[core, kept], sems, slot, to, col))
        slot += 1
    for copy in copies:
        copy.start()
    yield
    finish(copies)
    copy = remote(fin.at[core], fin.at[core], sems, slot, row, twin)
    copy.start()
    yield
    copy.wait()
    out_ref[:, :128] = fin[0].astype(jnp.float32)
    out_ref[:, 128:] = fin[1].astype(jnp.float32)


def reduce_scratch(nr, nz, total, classes, hidden):
    part = total // nr
    return [
        pltpu.VMEM((total, 128), jnp.float32),
        pltpu.VMEM((nr - 1, part, 128), jnp.float32),
        pltpu.VMEM((nz - 1, part // nz, 128), jnp.float32),
        pltpu.VMEM((2, total, 128), jnp.bfloat16),
        pltpu.VMEM((classes, hidden), jnp.float32),
        pltpu.VMEM((nr, classes, hidden), jnp.float32),
        pltpu.VMEM((nz, classes, hidden), jnp.float32),
        pltpu.SemaphoreType.DMA((2, 3 + 3 * (nr - 1) + 3 * (nz - 1))),
    ]


def present(down, right):
    row = lax.axis_index("row") + down
    col = lax.axis_index("col") + right
    rows = lax.axis_size("row")
    cols = lax.axis_size("col")
    return (row >= 0) & (row < rows) & (col >= 0) & (col < cols)


def greet_sides(barrier):
    row = lax.axis_index("row")
    col = lax.axis_index("col")
    for down, right in SIDES:

        @pl.when(present(down, right))
        def _():
            pl.semaphore_signal(barrier, inc=1, device_id=(row + down, col + right), device_id_type=MESH)


def count_sides():
    count = 0
    for down, right in SIDES:
        count = count + jnp.where(present(down, right), 1, 0)
    return count


def side_copies(cells, packs, rim_rows, rim_packs, sems, base, span):
    row = lax.axis_index("row")
    col = lax.axis_index("col")
    pixels = cells.shape[1]
    copies = []
    for index, (down, right) in enumerate(SIDES):
        if right == 0:
            source = cells.at[:, pl.ds(0 if down < 0 else pixels - span, span)]
            target = rim_rows.at[index]
        else:
            source = packs.at[0 if right < 0 else 1]
            target = rim_packs.at[index - 2]
        copies.append((down, right, remote(source, target, sems, base + index, row + down, col + right)))
    return copies


def start_sides(copies):
    for down, right, copy in copies:

        @pl.when(present(down, right))
        def _():
            copy.start()


def finish_sides(copies):
    for down, right, copy in copies:

        @pl.when(present(down, right))
        def _():
            copy.wait_send()

        @pl.when(present(-down, -right))
        def _():
            copy.wait_recv()


def clear_sides(rim_rows, rim_packs):
    for index, (down, right) in enumerate(SIDES):

        @pl.when(jnp.logical_not(present(-down, -right)))
        def _():
            if right == 0:
                rim_rows[index] = jnp.zeros(rim_rows.shape[1:], rim_rows.dtype)
            else:
                rim_packs[index - 2] = jnp.zeros(rim_packs.shape[1:], rim_packs.dtype)


def row_at(index, width):
    return pl.ds(pl.multiple_of(index * width, 128), width)


def pack_sides(cells, packs, rows, width, reach):
    lane = lax.broadcasted_iota(jnp.int32, (cells.shape[0], 128), 1)
    zero = jnp.zeros((cells.shape[0], 128), jnp.float32)

    def step(y, held):
        left = cells[:, pl.ds(pl.multiple_of(y * width, 128), 128)].astype(jnp.float32)
        right = cells[:, pl.ds(pl.multiple_of(y * width + width - 128, 128), 128)].astype(jnp.float32)
        here = (lane >= reach * y) & (lane < reach * y + reach)
        return (
            jnp.where(here, pltpu.roll(left, reach * y, 1), held[0]),
            jnp.where(here, pltpu.roll(right, lax.rem(reach * y + reach, 128), 1), held[1]),
        )

    held = lax.fori_loop(0, rows, step, (zero, zero))
    packs[0] = held[0].astype(packs.dtype)
    packs[1] = held[1].astype(packs.dtype)


def rim_tile(pack_left, pack_right, y, reach):
    lane = lax.broadcasted_iota(jnp.int32, pack_left.shape, 1)
    right = pltpu.roll(pack_right.astype(jnp.float32), lax.rem(128 - reach * y, 128), 1)
    left = pltpu.roll(pack_left.astype(jnp.float32), lax.rem(256 - reach - reach * y, 128), 1)
    return jnp.where(lane < reach, right, jnp.where(lane >= 128 - reach, left, 0.0))


def spread(cells, rim_rows, rim_packs, rows, width, reach, emit):
    def top(r, carry):
        tile = rim_tile(rim_packs[5], rim_packs[4], rows - reach + r, reach)
        wide = jnp.concatenate([rim_rows[1, :, row_at(r, width)].astype(jnp.float32), tile], axis=1)
        emit(r, wide)
        return carry

    def centre(r, carry):
        tile = rim_tile(rim_packs[1], rim_packs[0], r, reach)
        wide = jnp.concatenate([cells[:, row_at(r, width)].astype(jnp.float32), tile], axis=1)
        emit(r + reach, wide)
        return carry

    def bottom(r, carry):
        tile = rim_tile(rim_packs[3], rim_packs[2], r, reach)
        wide = jnp.concatenate([rim_rows[0, :, row_at(r, width)].astype(jnp.float32), tile], axis=1)
        emit(r + rows + reach, wide)
        return carry

    lax.fori_loop(0, reach, top, 0)
    lax.fori_loop(0, rows, centre, 0)
    lax.fori_loop(0, reach, bottom, 0)


def teacher_kernel(
    rows, width, feats, probs, refined, moved, weights, sweeps, moved_now, feat_packs, feat_rows, feat_rims,
    packs, prob_rows, prob_rims, sems,
):
    channels = feats.shape[0]
    span = REACH * width
    full_rows = rows * lax.axis_size("row")
    full_cols = width * lax.axis_size("col")
    first_row = lax.axis_index("row") * rows
    first_col = lax.axis_index("col") * width
    clear_sides(feat_rows, feat_rims)
    for sweep in range(ITERS):
        clear_sides(prob_rows.at[sweep], prob_rims.at[sweep])
    pack_sides(feats, feat_packs, rows, width, REACH)
    pack_sides(probs, packs.at[0], rows, width, REACH)
    barrier = pltpu.get_barrier_semaphore()
    greet_sides(barrier)
    pl.semaphore_wait(barrier, count_sides())
    feat_copies = side_copies(feats, feat_packs, feat_rows, feat_rims, sems, 0, span)
    start_sides(feat_copies)
    copies = side_copies(probs, packs.at[0], prob_rows.at[0], prob_rims.at[0], sems, 8, span)
    start_sides(copies)
    finish_sides(feat_copies)

    def emit_feats(r, wide):
        for index, shift in enumerate(SHIFTS):
            turned = wide if shift == 0 else pltpu.roll(wide, (-shift) % wide.shape[1], 1)
            moved[index, :, row_at(r, width)] = turned[:, :width]

    spread(feats, feat_rows, feat_rims, rows, width, REACH, emit_feats)
    place = first_col + lax.broadcasted_iota(jnp.int32, (8, width), 1)

    def weigh(y, carry):
        centre = moved[0, :, row_at(y + REACH, width)]
        total = jnp.ones((8, width), jnp.float32)
        terms = []
        for off_y, off_x in tap_list():
            other = moved[SHIFTS.index(off_x), :, row_at(y + REACH + off_y, width)]
            apart = (centre - other) * (centre - other)
            apart = jnp.sum(apart.reshape(channels // 8, 8, width), axis=0)
            apart = jnp.broadcast_to(jnp.sum(apart, axis=0, keepdims=True), (8, width))
            at_row = first_row + y + off_y
            inside = (place + off_x >= 0) & (place + off_x < full_cols) & (at_row >= 0) & (at_row < full_rows)
            term = jnp.where(inside, jnp.exp(apart * (-1.0 / channels)), 0.0)
            terms.append(term)
            total = total + term
        scale = 1.0 / total
        weights[0, :, row_at(y, width)] = scale
        for index, term in enumerate(terms):
            weights[index + 1, :, row_at(y, width)] = term * scale
        return carry

    lax.fori_loop(0, rows, weigh, 0)

    def emit_probs(r, wide):
        for index, shift in enumerate(SHIFTS):
            turned = wide if shift == 0 else pltpu.roll(wide, (-shift) % wide.shape[1], 1)
            moved_now[index, :, row_at(r, width)] = turned[:, :width]

    for sweep in range(ITERS):
        now = probs if sweep == 0 else sweeps.at[sweep - 1]
        later = refined if sweep == ITERS - 1 else sweeps.at[sweep]
        finish_sides(copies)
        spread(now, prob_rows.at[sweep], prob_rims.at[sweep], rows, width, REACH, emit_probs)

        def gather(y, carry):
            running = weights[0, :, row_at(y, width)] * moved_now[0, :, row_at(y + REACH, width)]
            for index, (off_y, off_x) in enumerate(tap_list()):
                running = running + (
                    weights[index + 1, :, row_at(y, width)]
                    * moved_now[SHIFTS.index(off_x), :, row_at(y + REACH + off_y, width)]
                )
            later[:, row_at(y, width)] = running
            return carry

        lax.fori_loop(0, rows, gather, 0)
        if sweep < ITERS - 1:
            pack_sides(later, packs.at[sweep + 1], rows, width, REACH)
            copies = side_copies(
                later, packs.at[sweep + 1], prob_rows.at[sweep + 1], prob_rims.at[sweep + 1], sems, 16 + 8 * sweep, span
            )
            start_sides(copies)


def refine(feats, probs, rows, width):
    channels, pixels = feats.shape
    classes = probs.shape[0]
    span = REACH * width
    wide = (rows + 2 * REACH) * width
    return pl.pallas_call(
        functools.partial(teacher_kernel, rows, width),
        out_shape=jax.ShapeDtypeStruct(probs.shape, jnp.float32),
        in_specs=[pl.BlockSpec(memory_space=pltpu.VMEM)] * 2,
        out_specs=pl.BlockSpec(memory_space=pltpu.VMEM),
        scratch_shapes=[
            pltpu.VMEM((len(SHIFTS), channels, wide), jnp.float32),
            pltpu.VMEM((25, 8, pixels), jnp.float32),
            pltpu.VMEM((ITERS - 1, classes, pixels), jnp.float32),
            pltpu.VMEM((len(SHIFTS), classes, wide), jnp.float32),
            pltpu.VMEM((2, channels, 128), jnp.bfloat16),
            pltpu.VMEM((2, channels, span), jnp.bfloat16),
            pltpu.VMEM((6, channels, 128), jnp.bfloat16),
            pltpu.VMEM((ITERS, 2, classes, 128), jnp.float32),
            pltpu.VMEM((ITERS, 2, classes, span), jnp.float32),
            pltpu.VMEM((ITERS, 6, classes, 128), jnp.float32),
            pltpu.SemaphoreType.DMA((2, 8 + 8 * ITERS)),
        ],
        compiler_params=pltpu.CompilerParams(collective_id=1, has_side_effects=True, vmem_limit_bytes=48 * 2**20),
    )(feats, probs)


def student_kernel(
    nr, nz, rows, width, scale, cells, ahead, back, class_in, class_out, refined,
    slope_grad, conv_out, class_grad,
    stacked, error, error_turned, error_stacked, parts, class_part,
    cell_packs, cell_rows, cell_rims, error_packs, error_rows, error_rims, side_sems, *reduce_refs,
):
    row = lax.axis_index("row")
    col = lax.axis_index("col")
    core = lax.rem(col, 2)
    z = col // 2
    channels, pixels = cells.shape
    clear_sides(cell_rows, cell_rims)
    clear_sides(error_rows, error_rims)
    pack_sides(cells, cell_packs, rows, width, 1)
    barrier = pltpu.get_barrier_semaphore()
    greet_sides(barrier)
    pl.semaphore_signal(barrier, inc=1, device_id=(row, z * 2 + 1 - core), device_id_type=MESH)
    for step in range(1, nr):
        pl.semaphore_signal(barrier, inc=1, device_id=(lax.rem(row + step, nr), col), device_id_type=MESH)
    for step in range(1, nz):
        pl.semaphore_signal(barrier, inc=1, device_id=(row, lax.rem(z + step, nz) * 2 + core), device_id_type=MESH)
    pl.semaphore_wait(barrier, count_sides() + (nr + nz - 1))
    copies = side_copies(cells, cell_packs, cell_rows, cell_rims, side_sems, 0, width)
    start_sides(copies)
    finish_sides(copies)

    def stack_into(target):
        depth = target.shape[0] // 3

        def emit(r, wide):
            for index, shift in enumerate((-1, 0, 1)):
                turned = wide if shift == 0 else pltpu.roll(wide, (-shift) % wide.shape[1], 1)
                target[index * depth : (index + 1) * depth, row_at(r, width)] = turned[:, :width].astype(target.dtype)

        return emit

    spread(cells, cell_rows, cell_rims, rows, width, 1, stack_into(stacked))
    class_part[...] = jnp.zeros_like(class_part)

    def forward(y, carry):
        here = row_at(y, width)
        pre = jnp.dot(ahead[0], stacked[:, here], preferred_element_type=jnp.float32)
        for tap_row in (1, 2):
            pre = pre + jnp.dot(
                ahead[tap_row], stacked[:, row_at(y + tap_row, width)], preferred_element_type=jnp.float32
            )
        gate = jax.nn.sigmoid(pre)
        hidden = (pre * gate).astype(jnp.bfloat16)
        logit = jnp.dot(class_in[...], hidden, preferred_element_type=jnp.float32)
        wrong = (jax.nn.sigmoid(logit) - refined[:, here]).astype(jnp.bfloat16)
        pull = jnp.dot(class_out[...], wrong, preferred_element_type=jnp.float32)
        slope = pull * (gate * (1.0 + pre * (1.0 - gate)))
        error[:, here] = slope.astype(jnp.bfloat16)
        error_turned[here, :] = slope.T.astype(jnp.bfloat16)
        class_part[...] += lax.dot_general(
            wrong, hidden, (((1,), (1,)), ((), ())), preferred_element_type=jnp.float32
        )
        return carry

    lax.fori_loop(0, rows, forward, 0)
    pack_sides(error, error_packs, rows, width, 1)
    copies = side_copies(error, error_packs, error_rows, error_rims, side_sems, 8, width)
    start_sides(copies)
    depth = stacked.shape[0]
    for tap_row in range(3):
        for index in range(3):
            block = pl.ds(index * channels, channels)
            parts[tap_row * depth + index * channels : tap_row * depth + (index + 1) * channels, :] = jnp.dot(
                stacked[block, tap_row * width : tap_row * width + pixels],
                error_turned[...],
                preferred_element_type=jnp.float32,
            )
    if parts.shape[0] > 3 * depth:
        parts[3 * depth :, :] = jnp.zeros((parts.shape[0] - 3 * depth, parts.shape[1]), jnp.float32)

    def features(y, carry):
        total = jnp.dot(back[0], error_stacked[:, row_at(y, width)], preferred_element_type=jnp.float32)
        for tap_row in (1, 2):
            total = total + jnp.dot(
                back[tap_row], error_stacked[:, row_at(y + tap_row, width)], preferred_element_type=jnp.float32
            )
        slope_grad[:, row_at(y, width)] = total.astype(jnp.bfloat16)
        return carry

    phases = reduce_body(nr, nz, scale, parts, class_part, conv_out, class_grad, *reduce_refs)
    for phase, _ in enumerate(phases):
        if phase == 0:
            finish_sides(copies)
        elif phase == 1:
            spread(error, error_rows, error_rims, rows, width, 1, stack_into(error_stacked))
            lax.fori_loop(0, rows, features, 0)


def student(cells, conv_weight, class_weight, refined, rows, width):
    channels, pixels = cells.shape
    hidden, classes = class_weight.shape
    nr = lax.axis_size("row")
    nz = lax.axis_size("col") // 2
    unit = nr * nz * 16
    wide = (rows + 2) * width
    total = -(-9 * channels // unit) * unit
    taps = conv_weight.reshape(3, 3, channels, hidden)
    ahead = taps.transpose(0, 3, 1, 2).reshape(3, hidden, 3 * channels)
    back = taps[::-1, ::-1].transpose(0, 2, 1, 3).reshape(3, channels, 3 * hidden)
    out = pl.pallas_call(
        functools.partial(student_kernel, nr, nz, rows, width, 1.0 / pixels),
        out_shape=(
            jax.ShapeDtypeStruct((channels, pixels), jnp.bfloat16),
            jax.ShapeDtypeStruct((total, hidden), jnp.float32),
            jax.ShapeDtypeStruct((classes, hidden), jnp.float32),
        ),
        in_specs=[pl.BlockSpec(memory_space=pltpu.VMEM)] * 6,
        out_specs=[pl.BlockSpec(memory_space=pltpu.VMEM)] * 3,
        scratch_shapes=[
            pltpu.VMEM((3 * channels, wide), jnp.bfloat16),
            pltpu.VMEM((hidden, pixels), jnp.bfloat16),
            pltpu.VMEM((pixels, hidden), jnp.bfloat16),
            pltpu.VMEM((3 * hidden, wide), jnp.bfloat16),
            pltpu.VMEM((total, hidden), jnp.float32),
            pltpu.VMEM((classes, hidden), jnp.float32),
            pltpu.VMEM((2, channels, 128), jnp.bfloat16),
            pltpu.VMEM((2, channels, width), jnp.bfloat16),
            pltpu.VMEM((6, channels, 128), jnp.bfloat16),
            pltpu.VMEM((2, hidden, 128), jnp.bfloat16),
            pltpu.VMEM((2, hidden, width), jnp.bfloat16),
            pltpu.VMEM((6, hidden, 128), jnp.bfloat16),
            pltpu.SemaphoreType.DMA((2, 16)),
        ]
        + reduce_scratch(nr, nz, total, classes, hidden),
        compiler_params=pltpu.CompilerParams(collective_id=0, has_side_effects=True, vmem_limit_bytes=56 * 2**20),
    )(cells, ahead, back, class_weight.T, class_weight, refined)
    return out[0], out[1][: 9 * channels], out[2]


def shards(teacher_feats, teacher_probs, student_feats, conv_weight, class_weight):
    classes, rows, width = teacher_probs.shape
    channels = student_feats.shape[0]
    pixels = rows * width
    refined = refine(
        teacher_feats.reshape(teacher_feats.shape[0], pixels), teacher_probs.reshape(classes, pixels), rows, width
    )
    feature_grad, grad_conv, grad_class = student(
        student_feats.reshape(channels, pixels), conv_weight, class_weight, refined, rows, width
    )
    return (
        refined.reshape(classes, rows, width),
        feature_grad.reshape(channels, rows, width),
        grad_conv.reshape(conv_weight.shape),
        grad_class.T,
    )


def solution(mesh):
    in_specs = (P(None, "row", "col"), P(None, "row", "col"), P(None, "row", "col"), P(), P())
    out_specs = (P(None, "row", "col"), P(None, "row", "col"), P(), P())
    return jax.shard_map(shards, mesh=mesh, in_specs=in_specs, out_specs=out_specs, check_vma=False)
```

profile of v0, /device:TPU:0, one launch (start us, length us, event | category | flops | bytes accessed | tf_op | source)
XLA Modules:
  0.0 169.3 jit_solution(12062077248928795658)
XLA Ops:
  0.6 0.0 copy-start.2
  0.6 1.3 copy.18
  2.0 1.0 copy.19
  2.9 56.5 %shard_map.84.refined = f32[8,4096]{1,0:T(8,128)S(1)} custom-call(bf16[64,4096]{1,0:T(8,128)(2,1)S(1)} %bitcast.20, f32[8,4096]{1,0:T(8,128)S(1)} %bitcast.22), custom_call_target="tpu_custom_call" | custom-call | tf_op jit(solution)/shard_map/pallas_call | solution.py:364
  59.5 0.0 copy-start
  59.5 0.6 copy-done
  60.1 0.0 copy-done.2
  60.1 0.1 reverse_bitcast_fusion
  60.2 0.7 copy.13
  61.0 1.6 copy.15.back
  62.5 3.8 %copy.20 = bf16[32,8,16,256]{3,1,2,0:T(8,128)(2,1)} copy(bf16[32,8,16,256]{3,2,1,0:T(8,128)(2,1)} %bitcast.28) | data formatting | bytes 4194304
  66.4 0.0 copy-start.4
  66.4 1.5 copy.14.ahead
  67.9 0.0 copy-done.4
  67.9 0.7 copy.16.class_out
  68.6 94.2 %shard_map.85 = (bf16[256,4096]{1,0:T(8,128)(2,1)}, f32[2304,256]{1,0:T(8,128)}, f32[8,256]{1,0:T(8,128)}) custom-call(bf16[256,4096]{1,0:T(8,128)(2,1)} %bitcast.23, bf16[3,256,768]{2,1,0:T(8,128)(2,1)} %copy.14.ahead, bf16[3,256,768]{2,1,0:T(8,128)(2,1)} %copy.15.back, bf16[8,256]{1,0:T(8,128)(2,1)} %bitcast.33, bf16[256,8]{1,0:T(8,128)(2,1)} %copy.16.class_out, ...), custom_call_target="tpu_custom_call" | custom-call | tf_op jit(solution)/shard_map/pallas_call | solution.py:490
  162.9 0.0 copy-start.1
  162.9 0.0 copy-start.3
  162.9 3.7 %copy.21 = bf16[32,8,16,256]{3,2,1,0:T(8,128)(2,1)} copy(bf16[32,8,16,256]{3,1,2,0:T(8,128)(2,1)} %bitcast.30) | data formatting | bytes 4194304
  166.6 0.0 copy-done.1
  166.6 0.7 copy.17
  167.3 0.0 copy-done.3
  167.3 0.0 copy-start.5
  167.3 1.4 copy.24
  168.7 0.0 copy-done.5
  168.7 0.6 copy.25
Async XLA Ops:
  0.6 59.5 %copy-start.2 = (bf16[9,256,256]{2,1,0:T(8,128)(2,1)S(1)}, bf16[9,256,256]{2,1,0:T(8,128)(2,1)}, u32[]{:S(2)}) copy-start(bf16[9,256,256]{2,1,0:T(8,128)(2,1)} %param.8) | copy-start | bytes 3538948
  59.5 0.7 copy-start
  66.4 1.5 copy-start.4
  162.9 3.7 %copy-start.1 = (f32[8,4096]{1,0:T(8,128)S(1)}, f32[8,4096]{1,0:T(8,128)}, u32[]{:S(2)}) copy-start(f32[8,4096]{1,0:T(8,128)} %copy-done) | copy-start | bytes 393220
  162.9 4.4 %copy-start.3 = (f32[2304,256]{1,0:T(8,128)S(1)}, f32[2304,256]{1,0:T(8,128)}, u32[]{:S(2)}) copy-start(f32[2304,256]{1,0:T(8,128)} %get-tuple-element.8) | copy-start | bytes 7077892
  167.3 1.4 copy-start.5
where the time goes:
time: 169 us
  Pallas kernels  151 us (89%)
  local copies, waits for them, and re-layouts  17.9 us (11%)
    pallas_call x1, Pallas kernels, student(): pl.pallas_call(functools.partial(student_kernel, nr, nz, rows, width, 1.0...  94.2 us
    pallas_call x1, Pallas kernels, refine(): pl.pallas_call(functools.partial(teacher_kernel, rows, width), out_shape=...  56.5 us
    unnamed x20, local copies, waits for them, and re-layouts  14 us

commit v1 on v0

v1 whole, which is shorter than its diff:
```python
import functools

import jax
import jax.numpy as jnp
from jax import lax
from jax.experimental import pallas as pl
from jax.experimental.pallas import tpu as pltpu
from jax.sharding import PartitionSpec as P

ITERS = 4
REACH = 4
SHIFTS = (0, 1, 2, 4, -1, -2, -4)
SIDES = ((-1, 0), (1, 0), (0, -1), (0, 1), (-1, -1), (-1, 1), (1, -1), (1, 1))


def tap_list():
    offsets = []
    for radius in (1, 2, 4):
        for step_y in (-1, 0, 1):
            for step_x in (-1, 0, 1):
                if step_y != 0 or step_x != 0:
                    offsets.append((step_y * radius, step_x * radius))
    return offsets


MESH = pl.DeviceIdType.MESH


def remote(src, dst, sems, slot, row, col):
    return pltpu.make_async_remote_copy(
        src_ref=src,
        dst_ref=dst,
        send_sem=sems.at[0, slot],
        recv_sem=sems.at[1, slot],
        device_id=(row, col),
        device_id_type=MESH,
    )


def finish(copies):
    for copy in copies:
        copy.wait()


def reduce_body(nr, nz, scale, g_ref, out_ref, core_buf, row_buf, z_buf, fin, sems, extra=None):
    if extra is not None:
        cls_ref, outc_ref, cls_core, cls_row, cls_z = extra
    row = lax.axis_index("row")
    col = lax.axis_index("col")
    core = lax.rem(col, 2)
    z = col // 2
    twin = z * 2 + 1 - core
    total = g_ref.shape[0]
    part = total // nr
    piece = part // nz
    mine = pl.ds(pl.multiple_of(core * 128, 128), 128)
    other = pl.ds(pl.multiple_of((1 - core) * 128, 128), 128)
    slot = 0
    copies = [remote(g_ref.at[:, other], core_buf, sems, 0, row, twin)]
    if extra is not None:
        copies.append(remote(cls_ref, cls_core, sems, 1, row, twin))
    for copy in copies:
        copy.start()
    yield
    finish(copies)
    slot = 2
    core_buf[...] = core_buf[...] + g_ref[:, mine]
    if extra is not None:
        cls_row[row] = cls_ref[...] + cls_core[...]
    copies = []
    for step in range(1, nr):
        to = lax.rem(row + step, nr)
        copies.append(
            remote(core_buf.at[pl.ds(pl.multiple_of(to * part, 16), part)], row_buf.at[step - 1], sems, slot, to, col)
        )
        if extra is not None:
            copies.append(remote(cls_row.at[row], cls_row.at[row], sems, slot + 1, to, col))
        slot += 2
    for copy in copies:
        copy.start()
    yield
    finish(copies)
    kept = pl.ds(pl.multiple_of(row * part, 16), part)
    summed = core_buf[kept]
    for step in range(1, nr):
        summed = summed + row_buf[step - 1]
    row_buf[0] = summed
    if extra is not None:
        across = cls_row[0]
        for i in range(1, nr):
            across = across + cls_row[i]
        cls_z[z] = across
    copies = []
    for step in range(1, nz):
        to = lax.rem(z + step, nz)
        copies.append(
            remote(row_buf.at[0, pl.ds(pl.multiple_of(to * piece, 16), piece)], z_buf.at[step - 1], sems, slot, row, to * 2 + core)
        )
        if extra is not None:
            copies.append(remote(cls_z.at[z], cls_z.at[z], sems, slot + 1, row, to * 2 + core))
        slot += 2
    for copy in copies:
        copy.start()
    yield
    finish(copies)
    summed = row_buf[0, pl.ds(pl.multiple_of(z * piece, 16), piece)]
    for step in range(1, nz):
        summed = summed + z_buf[step - 1]
    own = pl.ds(pl.multiple_of(row * part + z * piece, 16), piece)
    fin[core, own] = (summed * scale).astype(jnp.bfloat16)
    if extra is not None:
        across = cls_z[0]
        for i in range(1, nz):
            across = across + cls_z[i]
        outc_ref[...] = across * scale
    copies = []
    for step in range(1, nz):
        to = lax.rem(z + step, nz)
        copies.append(remote(fin.at[core, own], fin.at[core, own], sems, slot, row, to * 2 + core))
        slot += 1
    for copy in copies:
        copy.start()
    yield
    finish(copies)
    copies = []
    for step in range(1, nr):
        to = lax.rem(row + step, nr)
        copies.append(remote(fin.at[core, kept], fin.at[core, kept], sems, slot, to, col))
        slot += 1
    for copy in copies:
        copy.start()
    yield
    finish(copies)
    copy = remote(fin.at[core], fin.at[core], sems, slot, row, twin)
    copy.start()
    yield
    copy.wait()
    out_ref[:, :128] = fin[0].astype(jnp.float32)
    out_ref[:, 128:] = fin[1].astype(jnp.float32)


def reduce_scratch(nr, nz, total, classes, hidden):
    part = total // nr
    return [
        pltpu.VMEM((3, total, 128), jnp.float32),
        pltpu.VMEM((3, nr - 1, part, 128), jnp.float32),
        pltpu.VMEM((3, nz - 1, part // nz, 128), jnp.float32),
        pltpu.VMEM((3, 2, total, 128), jnp.bfloat16),
        pltpu.SemaphoreType.DMA((3, 2, 3 + 3 * (nr - 1) + 3 * (nz - 1))),
        pltpu.VMEM((classes, hidden), jnp.float32),
        pltpu.VMEM((nr, classes, hidden), jnp.float32),
        pltpu.VMEM((nz, classes, hidden), jnp.float32),
    ]


def present(down, right):
    row = lax.axis_index("row") + down
    col = lax.axis_index("col") + right
    rows = lax.axis_size("row")
    cols = lax.axis_size("col")
    return (row >= 0) & (row < rows) & (col >= 0) & (col < cols)


def greet_sides(barrier):
    row = lax.axis_index("row")
    col = lax.axis_index("col")
    for down, right in SIDES:

        @pl.when(present(down, right))
        def _():
            pl.semaphore_signal(barrier, inc=1, device_id=(row + down, col + right), device_id_type=MESH)


def count_sides():
    count = 0
    for down, right in SIDES:
        count = count + jnp.where(present(down, right), 1, 0)
    return count


def side_copies(cells, packs, rim_rows, rim_packs, sems, base, span):
    row = lax.axis_index("row")
    col = lax.axis_index("col")
    pixels = cells.shape[1]
    copies = []
    for index, (down, right) in enumerate(SIDES):
        if right == 0:
            source = cells.at[:, pl.ds(0 if down < 0 else pixels - span, span)]
            target = rim_rows.at[index]
        else:
            source = packs.at[0 if right < 0 else 1]
            target = rim_packs.at[index - 2]
        copies.append((down, right, remote(source, target, sems, base + index, row + down, col + right)))
    return copies


def start_sides(copies):
    for down, right, copy in copies:

        @pl.when(present(down, right))
        def _():
            copy.start()


def finish_sides(copies):
    for down, right, copy in copies:

        @pl.when(present(down, right))
        def _():
            copy.wait_send()

        @pl.when(present(-down, -right))
        def _():
            copy.wait_recv()


def clear_sides(rim_rows, rim_packs):
    for index, (down, right) in enumerate(SIDES):

        @pl.when(jnp.logical_not(present(-down, -right)))
        def _():
            if right == 0:
                rim_rows[index] = jnp.zeros(rim_rows.shape[1:], rim_rows.dtype)
            else:
                rim_packs[index - 2] = jnp.zeros(rim_packs.shape[1:], rim_packs.dtype)


def row_at(index, width):
    return pl.ds(pl.multiple_of(index * width, 128), width)


def pack_sides(cells, packs, rows, width, reach, unroll=1):
    lane = lax.broadcasted_iota(jnp.int32, (cells.shape[0], 128), 1)
    zero = jnp.zeros((cells.shape[0], 128), jnp.float32)

    def step(y, held):
        left = cells[:, pl.ds(pl.multiple_of(y * width, 128), 128)].astype(jnp.float32)
        right = cells[:, pl.ds(pl.multiple_of(y * width + width - 128, 128), 128)].astype(jnp.float32)
        here = (lane >= reach * y) & (lane < reach * y + reach)
        return (
            jnp.where(here, pltpu.roll(left, reach * y, 1), held[0]),
            jnp.where(here, pltpu.roll(right, lax.rem(reach * y + reach, 128), 1), held[1]),
        )

    held = lax.fori_loop(0, rows, step, (zero, zero), unroll=unroll)
    packs[0] = held[0].astype(packs.dtype)
    packs[1] = held[1].astype(packs.dtype)


def rim_tile(pack_left, pack_right, y, reach):
    lane = lax.broadcasted_iota(jnp.int32, pack_left.shape, 1)
    right = pltpu.roll(pack_right.astype(jnp.float32), lax.rem(128 - reach * y, 128), 1)
    left = pltpu.roll(pack_left.astype(jnp.float32), lax.rem(256 - reach - reach * y, 128), 1)
    return jnp.where(lane < reach, right, jnp.where(lane >= 128 - reach, left, 0.0))


def spread(cells, rim_rows, rim_packs, rows, width, reach, emit, unroll=1):
    def top(r, carry):
        tile = rim_tile(rim_packs[5], rim_packs[4], rows - reach + r, reach)
        wide = jnp.concatenate([rim_rows[1, :, row_at(r, width)].astype(jnp.float32), tile], axis=1)
        emit(r, wide)
        return carry

    def centre(r, carry):
        tile = rim_tile(rim_packs[1], rim_packs[0], r, reach)
        wide = jnp.concatenate([cells[:, row_at(r, width)].astype(jnp.float32), tile], axis=1)
        emit(r + reach, wide)
        return carry

    def bottom(r, carry):
        tile = rim_tile(rim_packs[3], rim_packs[2], r, reach)
        wide = jnp.concatenate([rim_rows[0, :, row_at(r, width)].astype(jnp.float32), tile], axis=1)
        emit(r + rows + reach, wide)
        return carry

    lax.fori_loop(0, reach, top, 0, unroll=min(unroll, reach))
    lax.fori_loop(0, rows, centre, 0, unroll=unroll)
    lax.fori_loop(0, reach, bottom, 0, unroll=min(unroll, reach))


def step_kernel(
    nr, nz, rows, width, scale,
    feats, probs, cells, ahead, back, class_in, class_out,
    refined, slope_grad, conv_out, class_grad,
    moved, weights, sweeps, moved_now, feat_packs, feat_rows, feat_rims, packs, prob_rows, prob_rims,
    stacked, steep, hidden_all, chance, error, error_turned, parts, class_part,
    cell_packs, cell_rows, cell_rims, error_packs, error_rows, error_rims, sems,
    core_buf, row_buf, z_buf, fin, reduce_sems, cls_core, cls_row, cls_z,
):
    row = lax.axis_index("row")
    col = lax.axis_index("col")
    core = lax.rem(col, 2)
    z = col // 2
    teacher_channels = feats.shape[0]
    channels, pixels = cells.shape
    hidden_size = class_out.shape[0]
    span = REACH * width
    full_rows = rows * lax.axis_size("row")
    full_cols = width * lax.axis_size("col")
    first_row = row * rows
    first_col = col * width

    barrier = pltpu.get_barrier_semaphore()
    clear_sides(feat_rows, feat_rims)
    clear_sides(cell_rows, cell_rims)
    clear_sides(error_rows, error_rims)
    for sweep in range(ITERS):
        clear_sides(prob_rows.at[sweep], prob_rims.at[sweep])
    greet_sides(barrier)
    pl.semaphore_signal(barrier, inc=1, device_id=(row, z * 2 + 1 - core), device_id_type=MESH)
    for step in range(1, nr):
        pl.semaphore_signal(barrier, inc=1, device_id=(lax.rem(row + step, nr), col), device_id_type=MESH)
    for step in range(1, nz):
        pl.semaphore_signal(barrier, inc=1, device_id=(row, lax.rem(z + step, nz) * 2 + core), device_id_type=MESH)
    pack_sides(feats, feat_packs, rows, width, REACH, 4)
    pack_sides(probs, packs.at[0], rows, width, REACH, rows)
    pl.semaphore_wait(barrier, count_sides() + (nr + nz - 1))
    feat_copies = side_copies(feats, feat_packs, feat_rows, feat_rims, sems, 0, span)
    start_sides(feat_copies)
    copies = side_copies(probs, packs.at[0], prob_rows.at[0], prob_rims.at[0], sems, 8, span)
    start_sides(copies)
    pack_sides(cells, cell_packs, rows, width, 1)
    base = 8 + 8 * ITERS
    cell_copies = side_copies(cells, cell_packs, cell_rows, cell_rims, sems, base, width)
    start_sides(cell_copies)
    finish_sides(feat_copies)

    def emit_feats(r, wide):
        for index, shift in enumerate(SHIFTS):
            turned = wide if shift == 0 else pltpu.roll(wide, (-shift) % wide.shape[1], 1)
            moved[index, :, row_at(r, width)] = turned[:, :width]

    spread(feats, feat_rows, feat_rims, rows, width, REACH, emit_feats)
    place = first_col + lax.broadcasted_iota(jnp.int32, (8, width), 1)

    def weigh(y, carry):
        centre = moved[0, :, row_at(y + REACH, width)]
        total = jnp.ones((8, width), jnp.float32)
        terms = []
        for off_y, off_x in tap_list():
            other = moved[SHIFTS.index(off_x), :, row_at(y + REACH + off_y, width)]
            apart = (centre - other) * (centre - other)
            apart = jnp.sum(apart.reshape(teacher_channels // 8, 8, width), axis=0)
            apart = jnp.broadcast_to(jnp.sum(apart, axis=0, keepdims=True), (8, width))
            at_row = first_row + y + off_y
            inside = (place + off_x >= 0) & (place + off_x < full_cols) & (at_row >= 0) & (at_row < full_rows)
            term = jnp.where(inside, jnp.exp(apart * (-1.0 / teacher_channels)), 0.0)
            terms.append(term)
            total = total + term
        share = 1.0 / total
        weights[0, :, row_at(y, width)] = share
        for index, term in enumerate(terms):
            weights[index + 1, :, row_at(y, width)] = term * share
        return carry

    lax.fori_loop(0, rows, weigh, 0)

    def emit_probs(r, wide):
        for index, shift in enumerate(SHIFTS):
            turned = wide if shift == 0 else pltpu.roll(wide, (-shift) % wide.shape[1], 1)
            moved_now[index, :, row_at(r, width)] = turned[:, :width]

    def stack_into(depth):
        def emit(r, wide):
            for index, shift in enumerate((-1, 0, 1)):
                turned = wide if shift == 0 else pltpu.roll(wide, (-shift) % wide.shape[1], 1)
                stacked[index * depth : (index + 1) * depth, row_at(r, width)] = turned[:, :width].astype(stacked.dtype)

        return emit

    def forward(y, carry):
        here = row_at(y, width)
        pre = jnp.dot(ahead[0], stacked[: 3 * channels, here], preferred_element_type=jnp.float32)
        for tap_row in (1, 2):
            pre = pre + jnp.dot(
                ahead[tap_row], stacked[: 3 * channels, row_at(y + tap_row, width)], preferred_element_type=jnp.float32
            )
        gate = jax.nn.sigmoid(pre)
        hidden = (pre * gate).astype(jnp.bfloat16)
        hidden_all[:, here] = hidden
        steep[:, here] = gate * (1.0 + pre * (1.0 - gate))
        logit = jnp.dot(class_in[...], hidden, preferred_element_type=jnp.float32)
        chance[:, here] = jax.nn.sigmoid(logit)
        return carry

    for sweep in range(ITERS):
        now = probs if sweep == 0 else sweeps.at[sweep - 1]
        later = refined if sweep == ITERS - 1 else sweeps.at[sweep]
        finish_sides(copies)
        spread(now, prob_rows.at[sweep], prob_rims.at[sweep], rows, width, REACH, emit_probs, rows)

        def gather(y, carry):
            running = weights[0, :, row_at(y, width)] * moved_now[0, :, row_at(y + REACH, width)]
            for index, (off_y, off_x) in enumerate(tap_list()):
                running = running + (
                    weights[index + 1, :, row_at(y, width)]
                    * moved_now[SHIFTS.index(off_x), :, row_at(y + REACH + off_y, width)]
                )
            later[:, row_at(y, width)] = running
            return carry

        lax.fori_loop(0, rows, gather, 0, unroll=2)
        if sweep < ITERS - 1:
            pack_sides(later, packs.at[sweep + 1], rows, width, REACH, rows)
            copies = side_copies(
                later, packs.at[sweep + 1], prob_rows.at[sweep + 1], prob_rims.at[sweep + 1], sems, 16 + 8 * sweep, span
            )
            start_sides(copies)
            if sweep == 0:
                finish_sides(cell_copies)
                spread(cells, cell_rows, cell_rims, rows, width, 1, stack_into(channels))
            elif sweep < ITERS - 2:
                lax.fori_loop(0, rows // 2, forward, 0)
            else:
                lax.fori_loop(rows // 2, rows, forward, 0)

    class_part[...] = jnp.zeros_like(class_part)

    def backward(y, carry):
        here = row_at(y, width)
        wrong = (chance[:, here] - refined[:, here]).astype(jnp.bfloat16)
        slope = jnp.dot(class_out[...], wrong, preferred_element_type=jnp.float32) * steep[:, here]
        error[:, here] = slope.astype(jnp.bfloat16)
        error_turned[here, :] = slope.T.astype(jnp.bfloat16)
        class_part[...] += lax.dot_general(
            wrong, hidden_all[:, here], (((1,), (1,)), ((), ())), preferred_element_type=jnp.float32
        )
        return carry

    lax.fori_loop(0, rows, backward, 0, unroll=2)

    def run_chunk(chunk):
        for index in range(3):
            parts[chunk, index * channels : (index + 1) * channels, :] = jnp.dot(
                stacked[index * channels : (index + 1) * channels, chunk * width : chunk * width + pixels],
                error_turned[...],
                preferred_element_type=jnp.float32,
            )
        if parts.shape[1] > 3 * channels:
            parts[chunk, 3 * channels :, :] = jnp.zeros((parts.shape[1] - 3 * channels, parts.shape[2]), jnp.float32)

    def features(y, carry):
        total = jnp.dot(back[0], stacked[: 3 * hidden_size, row_at(y, width)], preferred_element_type=jnp.float32)
        for tap_row in (1, 2):
            total = total + jnp.dot(
                back[tap_row], stacked[: 3 * hidden_size, row_at(y + tap_row, width)], preferred_element_type=jnp.float32
            )
        slope_grad[:, row_at(y, width)] = total.astype(jnp.bfloat16)
        return carry

    def chunk_phases(chunk):
        extra = (class_part, class_grad, cls_core, cls_row, cls_z) if chunk == 0 else None
        return reduce_body(
            nr, nz, scale, parts.at[chunk], conv_out.at[chunk], core_buf.at[chunk], row_buf.at[chunk],
            z_buf.at[chunk], fin.at[chunk], reduce_sems.at[chunk], extra,
        )

    phases = [chunk_phases(chunk) for chunk in range(3)]
    run_chunk(0)
    next(phases[0])
    pack_sides(error, error_packs, rows, width, 1)
    copies = side_copies(error, error_packs, error_rows, error_rims, sems, base + 8, width)
    start_sides(copies)
    run_chunk(1)
    next(phases[0])
    next(phases[1])
    run_chunk(2)
    next(phases[1])
    next(phases[2])
    finish_sides(copies)
    spread(error, error_rows, error_rims, rows, width, 1, stack_into(hidden_size))
    turn = 0
    while phases:
        phases = [phase for phase in phases if next(phase, True) is None]
        if turn < 4:
            lax.fori_loop(turn * rows // 4, (turn + 1) * rows // 4, features, 0)
        turn += 1


def whole_step(feats, probs, cells, conv_weight, class_weight, rows, width):
    teacher_channels = feats.shape[0]
    channels, pixels = cells.shape
    hidden, classes = class_weight.shape
    nr = lax.axis_size("row")
    nz = lax.axis_size("col") // 2
    unit = nr * nz * 16
    span = REACH * width
    wide = (rows + 2) * width
    wider = (rows + 2 * REACH) * width
    total = -(-3 * channels // unit) * unit
    taps = conv_weight.reshape(3, 3, channels, hidden)
    ahead = taps.transpose(0, 3, 1, 2).reshape(3, hidden, 3 * channels)
    back = taps[::-1, ::-1].transpose(0, 2, 1, 3).reshape(3, channels, 3 * hidden)
    f32, bf16 = jnp.float32, jnp.bfloat16
    out = pl.pallas_call(
        functools.partial(step_kernel, nr, nz, rows, width, 1.0 / pixels),
        out_shape=(
            jax.ShapeDtypeStruct((classes, pixels), f32),
            jax.ShapeDtypeStruct((channels, pixels), bf16),
            jax.ShapeDtypeStruct((3, total, hidden), f32),
            jax.ShapeDtypeStruct((classes, hidden), f32),
        ),
        in_specs=[pl.BlockSpec(memory_space=pltpu.VMEM)] * 7,
        out_specs=[pl.BlockSpec(memory_space=pltpu.VMEM)] * 4,
        scratch_shapes=[
            pltpu.VMEM((len(SHIFTS), teacher_channels, wider), f32),
            pltpu.VMEM((25, 8, pixels), f32),
            pltpu.VMEM((ITERS - 1, classes, pixels), f32),
            pltpu.VMEM((len(SHIFTS), classes, wider), f32),
            pltpu.VMEM((2, teacher_channels, 128), bf16),
            pltpu.VMEM((2, teacher_channels, span), bf16),
            pltpu.VMEM((6, teacher_channels, 128), bf16),
            pltpu.VMEM((ITERS, 2, classes, 128), f32),
            pltpu.VMEM((ITERS, 2, classes, span), f32),
            pltpu.VMEM((ITERS, 6, classes, 128), f32),
            pltpu.VMEM((3 * max(channels, hidden), wide), bf16),
            pltpu.VMEM((hidden, pixels), f32),
            pltpu.VMEM((hidden, pixels), bf16),
            pltpu.VMEM((classes, pixels), f32),
            pltpu.VMEM((hidden, pixels), bf16),
            pltpu.VMEM((pixels, hidden), bf16),
            pltpu.VMEM((3, total, hidden), f32),
            pltpu.VMEM((classes, hidden), f32),
            pltpu.VMEM((2, channels, 128), bf16),
            pltpu.VMEM((2, channels, width), bf16),
            pltpu.VMEM((6, channels, 128), bf16),
            pltpu.VMEM((2, hidden, 128), bf16),
            pltpu.VMEM((2, hidden, width), bf16),
            pltpu.VMEM((6, hidden, 128), bf16),
            pltpu.SemaphoreType.DMA((2, 24 + 8 * ITERS)),
        ]
        + reduce_scratch(nr, nz, total, classes, hidden),
        compiler_params=pltpu.CompilerParams(collective_id=0, has_side_effects=True, vmem_limit_bytes=60 * 2**20),
    )(feats, probs, cells, ahead, back, class_weight.T, class_weight)
    return out[0], out[1], out[2][:, : 3 * channels], out[3]


def shards(teacher_feats, teacher_probs, student_feats, conv_weight, class_weight):
    classes, rows, width = teacher_probs.shape
    channels = student_feats.shape[0]
    pixels = rows * width
    refined, feature_grad, grad_conv, grad_class = whole_step(
        teacher_feats.reshape(teacher_feats.shape[0], pixels),
        teacher_probs.reshape(classes, pixels),
        student_feats.reshape(channels, pixels),
        conv_weight,
        class_weight,
        rows,
        width,
    )
    return (
        refined.reshape(classes, rows, width),
        feature_grad.reshape(channels, rows, width),
        grad_conv.reshape(conv_weight.shape),
        grad_class.T,
    )


def solution(mesh):
    in_specs = (P(None, "row", "col"), P(None, "row", "col"), P(None, "row", "col"), P(), P())
    out_specs = (P(None, "row", "col"), P(None, "row", "col"), P(), P())
    return jax.shard_map(shards, mesh=mesh, in_specs=in_specs, out_specs=out_specs, check_vma=False)
```

time: 169 us -> 123 us (0.73)
  Pallas kernels: 151 us -> 103 us
    pallas_call x2 -> x1, Pallas kernels: 151 us -> 103 us  [whole_step(): pl.pallas_call(functools.partial(step_kernel, nr, nz, rows, width, 1.0 /...]
    unnamed x20 -> x16, local copies, waits for them, and re-layouts: 14 us -> 15.2 us
where the time goes in v1:
time: 123 us
  Pallas kernels  103 us (84%)
  local copies, waits for them, and re-layouts  19.1 us (16%)
    pallas_call x1, Pallas kernels, whole_step(): pl.pallas_call(functools.partial(step_kernel, nr, nz, rows, width, 1.0 /...  103 us
    unnamed x16, local copies, waits for them, and re-layouts  15.2 us

profile of v1, /device:TPU:0, one launch (start us, length us, event | category | flops | bytes accessed | tf_op | source)
XLA Modules:
  0.0 123.2 jit_solution(5169196232065895472)
XLA Ops:
  0.6 0.0 copy-start
  0.6 1.5 %copy.16.class_out = bf16[256,8]{1,0:T(8,128)(2,1)} copy(bf16[256,8]{0,1:T(8,128)(2,1)} %param.9) | data formatting | bytes 8192 | tf_op args[4]
  2.2 1.6 %copy.19 = f32[1,8,16,256]{3,1,2,0:T(8,128)} copy(f32[1,8,16,256]{3,2,1,0:T(8,128)} %bitcast.31) | data formatting | bytes 262144
  3.8 2.0 %copy.18 = bf16[8,8,16,256]{3,1,2,0:T(8,128)(2,1)} copy(bf16[8,8,16,256]{3,2,1,0:T(8,128)(2,1)} %bitcast.30) | data formatting | bytes 1048576
  5.8 0.0 copy-done
  5.8 0.1 reverse_bitcast_fusion
  5.9 0.7 copy.13
  6.7 1.6 %copy.15.back = bf16[3,256,768]{2,1,0:T(8,128)(2,1)} copy(bf16[3,256,768]{1,2,0:T(8,128)(2,1)S(1)} %bitcast.23) | data formatting | bytes 2359296 | tf_op jit(solution)/shard_map/reshape | solution.py:493
  8.2 0.0 copy-start.2
  8.2 1.5 %copy.14.ahead = bf16[3,256,768]{2,1,0:T(8,128)(2,1)} copy(bf16[3,256,768]{1,2,0:T(8,128)(2,1)S(1)} %bitcast.22) | data formatting | bytes 2359296 | tf_op jit(solution)/shard_map/reshape | solution.py:492
  9.7 0.4 copy-done.2
  10.2 2.2 %copy.20 = bf16[32,8,16,256]{3,1,2,0:T(8,128)(2,1)} copy(bf16[32,8,16,256]{3,2,1,0:T(8,128)(2,1)S(1)} %bitcast.26) | data formatting | bytes 4194304
  12.4 103.4 %shard_map.84 = (f32[8,4096]{1,0:T(8,128)}, bf16[256,4096]{1,0:T(8,128)(2,1)}, f32[3,768,256]{2,1,0:T(8,128)}, f32[8,256]{1,0:T(8,128)}) custom-call(bf16[64,4096]{1,0:T(8,128)(2,1)} %bitcast.25, f32[8,4096]{1,0:T(8,128)} %bitcast.29, bf16[256,4096]{1,0:T(8,128)(2,1)} %bitcast.20, bf16[3,256,768]{2,1,0:T(8,128)(2,1)} %copy.14.ahead, ...), custom_call_target="tpu_custom_call" | custom-call | tf_op jit(solution)/shard_map/pallas_call | solution.py:495
  115.8 1.6 %copy.17 = f32[8,16,256]{2,1,0:T(8,128)} copy(f32[8,16,256]{2,0,1:T(8,128)} %bitcast.32) | data formatting | bytes 262144
  117.4 0.0 copy-start.1
  117.4 3.7 %copy.21 = bf16[32,8,16,256]{3,2,1,0:T(8,128)(2,1)} copy(bf16[32,8,16,256]{3,1,2,0:T(8,128)(2,1)} %bitcast.27) | data formatting | bytes 4194304
  121.2 0.0 copy-done.1
  121.2 0.0 copy-start.3
  121.2 1.4 %copy.24 = f32[9,256,256]{2,1,0:T(8,128)} copy(f32[9,256,256]{2,1,0:T(8,128)S(1)} %bitcast.24) | data formatting | bytes 4718592
  122.6 0.0 copy-done.3
  122.6 0.6 copy.25
Async XLA Ops:
  0.6 5.2 %copy-start = (bf16[9,256,256]{2,1,0:T(8,128)(2,1)S(1)}, bf16[9,256,256]{2,1,0:T(8,128)(2,1)}, u32[]{:S(2)}) copy-start(bf16[9,256,256]{2,1,0:T(8,128)(2,1)} %param.8) | copy-start | bytes 3538948
  8.2 2.0 %copy-start.2 = (bf16[256,16,256]{2,1,0:T(8,128)(2,1)S(1)}, bf16[256,16,256]{2,1,0:T(8,128)(2,1)}, u32[]{:S(2)}) copy-start(bf16[256,16,256]{2,1,0:T(8,128)(2,1)} %param.7) | copy-start | bytes 6291460
  117.4 3.7 %copy-start.1 = (f32[3,768,256]{2,1,0:T(8,128)S(1)}, f32[3,768,256]{2,1,0:T(8,128)}, u32[]{:S(2)}) copy-start(f32[3,768,256]{2,1,0:T(8,128)} %get-tuple-element.10) | copy-start | bytes 7077892
  121.2 1.4 %copy-start.3 = (f32[8,256]{1,0:T(8,128)S(1)}, f32[8,256]{1,0:T(8,128)}, u32[]{:S(2)}) copy-start(f32[8,256]{1,0:T(8,128)} %get-tuple-element.11) | copy-start | bytes 24580

commit v2 on v1

--- a/solution.py
+++ b/solution.py
@@ -247,6 +247,18 @@
     packs[1] = held[1].astype(packs.dtype)
 
 
+def turn_packs(packs, turned):
+    for side in range(2):
+        turned[side] = packs[side].T[: turned.shape[1]].astype(turned.dtype)
+
+
+def unturn_rims(turned, rim_packs):
+    for index in range(6):
+        rows = turned[index].astype(jnp.float32)
+        rest = jnp.zeros((128 - rows.shape[0], rows.shape[1]), jnp.float32)
+        rim_packs[index] = jnp.concatenate([rows, rest], axis=0).T
+
+
 def rim_tile(pack_left, pack_right, y, reach):
     lane = lax.broadcasted_iota(jnp.int32, pack_left.shape, 1)
     right = pltpu.roll(pack_right.astype(jnp.float32), lax.rem(128 - reach * y, 128), 1)
@@ -280,9 +292,9 @@
 
 def step_kernel(
     nr, nz, rows, width, scale,
-    feats, probs, cells, ahead, back, class_in, class_out,
+    feats, probs, cells, conv_weight, class_in,
     refined, slope_grad, conv_out, class_grad,
-    moved, weights, sweeps, moved_now, feat_packs, feat_rows, feat_rims, packs, prob_rows, prob_rims,
+    ahead, back, class_out, wide_packs, wide_rims, moved, weights, sweeps, moved_now, feat_packs, feat_rows, feat_rims, packs, prob_rows, prob_rims,
     stacked, steep, hidden_all, chance, error, error_turned, parts, class_part,
     cell_packs, cell_rows, cell_rims, error_packs, error_rows, error_rims, sems,
     core_buf, row_buf, z_buf, fin, reduce_sems, cls_core, cls_row, cls_z,
@@ -293,7 +305,7 @@
     z = col // 2
     teacher_channels = feats.shape[0]
     channels, pixels = cells.shape
-    hidden_size = class_out.shape[0]
+    hidden_size = class_in.shape[1]
     span = REACH * width
     full_rows = rows * lax.axis_size("row")
     full_cols = width * lax.axis_size("col")
@@ -319,10 +331,18 @@
     start_sides(feat_copies)
     copies = side_copies(probs, packs.at[0], prob_rows.at[0], prob_rims.at[0], sems, 8, span)
     start_sides(copies)
-    pack_sides(cells, cell_packs, rows, width, 1)
+    pack_sides(cells, wide_packs, rows, width, 1)
+    turn_packs(wide_packs, cell_packs)
     base = 8 + 8 * ITERS
     cell_copies = side_copies(cells, cell_packs, cell_rows, cell_rims, sems, base, width)
     start_sides(cell_copies)
+    for tap in range(9):
+        index = tap % 3
+        ahead[tap // 3, :, index * channels : (index + 1) * channels] = (
+            conv_weight[tap].astype(jnp.float32).T.astype(jnp.bfloat16)
+        )
+        back[tap // 3, :, index * hidden_size : (index + 1) * hidden_size] = conv_weight[8 - tap]
+    class_out[...] = class_in[...].astype(jnp.float32).T.astype(jnp.bfloat16)
     finish_sides(feat_copies)
 
     def emit_feats(r, wide):
@@ -408,7 +428,8 @@
             start_sides(copies)
             if sweep == 0:
                 finish_sides(cell_copies)
-                spread(cells, cell_rows, cell_rims, rows, width, 1, stack_into(channels))
+                unturn_rims(cell_rims, wide_rims)
+                spread(cells, cell_rows, wide_rims, rows, width, 1, stack_into(channels))
             elif sweep < ITERS - 2:
                 lax.fori_loop(0, rows // 2, forward, 0)
             else:
@@ -456,11 +477,12 @@
         )
 
     phases = [chunk_phases(chunk) for chunk in range(3)]
+    pack_sides(error, wide_packs, rows, width, 1)
+    turn_packs(wide_packs, error_packs)
+    copies = side_copies(error, error_packs, error_rows, error_rims, sems, base + 8, width)
+    start_sides(copies)
     run_chunk(0)
     next(phases[0])
-    pack_sides(error, error_packs, rows, width, 1)
-    copies = side_copies(error, error_packs, error_rows, error_rims, sems, base + 8, width)
-    start_sides(copies)
     run_chunk(1)
     next(phases[0])
     next(phases[1])
@@ -468,7 +490,8 @@
     next(phases[1])
     next(phases[2])
     finish_sides(copies)
-    spread(error, error_rows, error_rims, rows, width, 1, stack_into(hidden_size))
+    unturn_rims(error_rims, wide_rims)
+    spread(error, error_rows, wide_rims, rows, width, 1, stack_into(hidden_size))
     turn = 0
     while phases:
         phases = [phase for phase in phases if next(phase, True) is None]
@@ -488,9 +511,7 @@
     wide = (rows + 2) * width
     wider = (rows + 2 * REACH) * width
     total = -(-3 * channels // unit) * unit
-    taps = conv_weight.reshape(3, 3, channels, hidden)
-    ahead = taps.transpose(0, 3, 1, 2).reshape(3, hidden, 3 * channels)
-    back = taps[::-1, ::-1].transpose(0, 2, 1, 3).reshape(3, channels, 3 * hidden)
+    turned = -(-rows // 16) * 16
     f32, bf16 = jnp.float32, jnp.bfloat16
     out = pl.pallas_call(
         functools.partial(step_kernel, nr, nz, rows, width, 1.0 / pixels),
@@ -500,9 +521,14 @@
             jax.ShapeDtypeStruct((3, total, hidden), f32),
             jax.ShapeDtypeStruct((classes, hidden), f32),
         ),
-        in_specs=[pl.BlockSpec(memory_space=pltpu.VMEM)] * 7,
+        in_specs=[pl.BlockSpec(memory_space=pltpu.VMEM)] * 5,
         out_specs=[pl.BlockSpec(memory_space=pltpu.VMEM)] * 4,
         scratch_shapes=[
+            pltpu.VMEM((3, hidden, 3 * channels), bf16),
+            pltpu.VMEM((3, channels, 3 * hidden), bf16),
+            pltpu.VMEM((hidden, classes), bf16),
+            pltpu.VMEM((2, max(channels, hidden), 128), f32),
+            pltpu.VMEM((6, max(channels, hidden), 128), f32),
             pltpu.VMEM((len(SHIFTS), teacher_channels, wider), f32),
             pltpu.VMEM((25, 8, pixels), f32),
             pltpu.VMEM((ITERS - 1, classes, pixels), f32),
@@ -521,17 +547,17 @@
             pltpu.VMEM((pixels, hidden), bf16),
             pltpu.VMEM((3, total, hidden), f32),
             pltpu.VMEM((classes, hidden), f32),
-            pltpu.VMEM((2, channels, 128), bf16),
+            pltpu.VMEM((2, turned, channels), bf16),
             pltpu.VMEM((2, channels, width), bf16),
-            pltpu.VMEM((6, channels, 128), bf16),
-            pltpu.VMEM((2, hidden, 128), bf16),
+            pltpu.VMEM((6, turned, channels), bf16),
+            pltpu.VMEM((2, turned, hidden), bf16),
             pltpu.VMEM((2, hidden, width), bf16),
-            pltpu.VMEM((6, hidden, 128), bf16),
+            pltpu.VMEM((6, turned, hidden), bf16),
             pltpu.SemaphoreType.DMA((2, 24 + 8 * ITERS)),
         ]
         + reduce_scratch(nr, nz, total, classes, hidden),
         compiler_params=pltpu.CompilerParams(collective_id=0, has_side_effects=True, vmem_limit_bytes=60 * 2**20),
-    )(feats, probs, cells, ahead, back, class_weight.T, class_weight)
+    )(feats, probs, cells, conv_weight, class_weight.T)
     return out[0], out[1], out[2][:, : 3 * channels], out[3]
 
 

time: 123 us -> 111 us (0.902)
  Pallas kernels: 103 us -> 95.1 us
  local copies, waits for them, and re-layouts: 19.1 us -> 14.8 us
    pallas_call x1, Pallas kernels: 103 us -> 95.1 us  [whole_step(): pl.pallas_call(functools.partial(step_kernel, nr, nz, rows, width, 1.0 /...]
    reshape x2 -> x0, local copies, waits for them, and re-layouts: 3.08 us -> none  [the longest x1 1.55 us: whole_step(): taps[::-1, ::-1].transpose(0, 2, 1, 3).reshape(3, channels, 3 * hidden)]
    unnamed x16 -> x11, local copies, waits for them, and re-layouts: 15.2 us -> 14.8 us
where the time goes in v2:
time: 111 us
  Pallas kernels  95.1 us (86%)
  local copies, waits for them, and re-layouts  14.8 us (13%)
    pallas_call x1, Pallas kernels, whole_step(): pl.pallas_call(functools.partial(step_kernel, nr, nz, rows, width, 1.0 /...  95.1 us
    unnamed x11, local copies, waits for them, and re-layouts  14.8 us

profile of v2, /device:TPU:0, one launch (start us, length us, event | category | flops | bytes accessed | tf_op | source)
XLA Modules:
  0.0 110.6 jit_solution(16483497234882742543)
XLA Ops:
  0.6 1.6 %copy.11 = f32[1,8,16,256]{3,1,2,0:T(8,128)} copy(f32[1,8,16,256]{3,2,1,0:T(8,128)} %bitcast.20) | data formatting | bytes 262144
  2.3 2.0 %copy.10 = bf16[8,8,16,256]{3,1,2,0:T(8,128)(2,1)} copy(bf16[8,8,16,256]{3,2,1,0:T(8,128)(2,1)} %bitcast.19) | data formatting | bytes 1048576
  4.3 3.8 %copy.12 = bf16[32,8,16,256]{3,1,2,0:T(8,128)(2,1)} copy(bf16[32,8,16,256]{3,2,1,0:T(8,128)(2,1)} %bitcast.15) | data formatting | bytes 4194304
  8.1 95.1 %shard_map.84 = (f32[8,4096]{1,0:T(8,128)}, bf16[256,4096]{1,0:T(8,128)(2,1)}, f32[3,768,256]{2,1,0:T(8,128)}, f32[8,256]{1,0:T(8,128)}) custom-call(bf16[64,4096]{1,0:T(8,128)(2,1)} %bitcast.14, f32[8,4096]{1,0:T(8,128)} %bitcast.18, bf16[256,4096]{1,0:T(8,128)(2,1)} %bitcast.12, bf16[9,256,256]{2,1,0:T(8,128)(2,1)} %conv_weight.1, bf16[8,256]{1,0:T(8,128)(2,1)} %bitcast.23), custom_call_target="tpu_custom_call" | custom-call | tf_op jit(solution)/shard_map/pallas_call | solution.py:516
  103.3 1.6 %copy.9 = f32[8,16,256]{2,1,0:T(8,128)} copy(f32[8,16,256]{2,0,1:T(8,128)} %bitcast.21) | data formatting | bytes 262144
  104.9 0.0 copy-start
  104.9 3.7 %copy.13 = bf16[32,8,16,256]{3,2,1,0:T(8,128)(2,1)} copy(bf16[32,8,16,256]{3,1,2,0:T(8,128)(2,1)} %bitcast.17) | data formatting | bytes 4194304
  108.6 0.0 copy-done
  108.6 0.0 copy-start.1
  108.6 1.4 %copy.16 = f32[9,256,256]{2,1,0:T(8,128)} copy(f32[9,256,256]{2,1,0:T(8,128)S(1)} %bitcast.13) | data formatting | bytes 4718592
  110.0 0.0 copy-done.1
  110.0 0.6 copy.17
Async XLA Ops:
  104.9 3.7 %copy-start = (f32[3,768,256]{2,1,0:T(8,128)S(1)}, f32[3,768,256]{2,1,0:T(8,128)}, u32[]{:S(2)}) copy-start(f32[3,768,256]{2,1,0:T(8,128)} %get-tuple-element.10) | copy-start | bytes 7077892
  108.6 1.4 %copy-start.1 = (f32[8,256]{1,0:T(8,128)S(1)}, f32[8,256]{1,0:T(8,128)}, u32[]{:S(2)}) copy-start(f32[8,256]{1,0:T(8,128)} %get-tuple-element.11) | copy-start | bytes 24580

commit v3 on v2

--- a/solution.py
+++ b/solution.py
@@ -350,7 +350,7 @@
             turned = wide if shift == 0 else pltpu.roll(wide, (-shift) % wide.shape[1], 1)
             moved[index, :, row_at(r, width)] = turned[:, :width]
 
-    spread(feats, feat_rows, feat_rims, rows, width, REACH, emit_feats)
+    spread(feats, feat_rows, feat_rims, rows, width, REACH, emit_feats, 2)
     place = first_col + lax.broadcasted_iota(jnp.int32, (8, width), 1)
 
     def weigh(y, carry):
@@ -431,9 +431,9 @@
                 unturn_rims(cell_rims, wide_rims)
                 spread(cells, cell_rows, wide_rims, rows, width, 1, stack_into(channels))
             elif sweep < ITERS - 2:
-                lax.fori_loop(0, rows // 2, forward, 0)
+                lax.fori_loop(0, rows // 2, forward, 0, unroll=2)
             else:
-                lax.fori_loop(rows // 2, rows, forward, 0)
+                lax.fori_loop(rows // 2, rows, forward, 0, unroll=2)
 
     class_part[...] = jnp.zeros_like(class_part)
 
@@ -496,7 +496,7 @@
     while phases:
         phases = [phase for phase in phases if next(phase, True) is None]
         if turn < 4:
-            lax.fori_loop(turn * rows // 4, (turn + 1) * rows // 4, features, 0)
+            lax.fori_loop(turn * rows // 4, (turn + 1) * rows // 4, features, 0, unroll=2)
         turn += 1
 
 

time: 111 us -> 114 us (1.027)
  Pallas kernels: 95.1 us -> 98.1 us
    pallas_call x1, Pallas kernels: 95.1 us -> 98.1 us  [whole_step(): pl.pallas_call(functools.partial(step_kernel, nr, nz, rows, width, 1.0 /...]
where the time goes in v3:
time: 114 us
  Pallas kernels  98.1 us (86%)
  local copies, waits for them, and re-layouts  14.8 us (13%)
    pallas_call x1, Pallas kernels, whole_step(): pl.pallas_call(functools.partial(step_kernel, nr, nz, rows, width, 1.0 /...  98.1 us
    unnamed x11, local copies, waits for them, and re-layouts  14.8 us

profile of v3, /device:TPU:0, one launch (start us, length us, event | category | flops | bytes accessed | tf_op | source)
XLA Modules:
  0.0 113.6 jit_solution(12902822368102383845)
XLA Ops:
  0.6 1.6 %copy.11 = f32[1,8,16,256]{3,1,2,0:T(8,128)} copy(f32[1,8,16,256]{3,2,1,0:T(8,128)} %bitcast.20) | data formatting | bytes 262144
  2.3 2.0 %copy.10 = bf16[8,8,16,256]{3,1,2,0:T(8,128)(2,1)} copy(bf16[8,8,16,256]{3,2,1,0:T(8,128)(2,1)} %bitcast.19) | data formatting | bytes 1048576
  4.3 3.8 %copy.12 = bf16[32,8,16,256]{3,1,2,0:T(8,128)(2,1)} copy(bf16[32,8,16,256]{3,2,1,0:T(8,128)(2,1)} %bitcast.15) | data formatting | bytes 4194304
  8.1 98.1 %shard_map.84 = (f32[8,4096]{1,0:T(8,128)}, bf16[256,4096]{1,0:T(8,128)(2,1)}, f32[3,768,256]{2,1,0:T(8,128)}, f32[8,256]{1,0:T(8,128)}) custom-call(bf16[64,4096]{1,0:T(8,128)(2,1)} %bitcast.14, f32[8,4096]{1,0:T(8,128)} %bitcast.18, bf16[256,4096]{1,0:T(8,128)(2,1)} %bitcast.12, bf16[9,256,256]{2,1,0:T(8,128)(2,1)} %conv_weight.1, bf16[8,256]{1,0:T(8,128)(2,1)} %bitcast.23), custom_call_target="tpu_custom_call" | custom-call | tf_op jit(solution)/shard_map/pallas_call | solution.py:516
  106.2 1.6 %copy.9 = f32[8,16,256]{2,1,0:T(8,128)} copy(f32[8,16,256]{2,0,1:T(8,128)} %bitcast.21) | data formatting | bytes 262144
  107.8 0.0 copy-start
  107.8 3.7 %copy.13 = bf16[32,8,16,256]{3,2,1,0:T(8,128)(2,1)} copy(bf16[32,8,16,256]{3,1,2,0:T(8,128)(2,1)} %bitcast.17) | data formatting | bytes 4194304
  111.6 0.0 copy-done
  111.6 0.0 copy-start.1
  111.6 1.4 %copy.16 = f32[9,256,256]{2,1,0:T(8,128)} copy(f32[9,256,256]{2,1,0:T(8,128)S(1)} %bitcast.13) | data formatting | bytes 4718592
  113.0 0.0 copy-done.1
  113.0 0.6 copy.17
Async XLA Ops:
  107.8 3.7 %copy-start = (f32[3,768,256]{2,1,0:T(8,128)S(1)}, f32[3,768,256]{2,1,0:T(8,128)}, u32[]{:S(2)}) copy-start(f32[3,768,256]{2,1,0:T(8,128)} %get-tuple-element.10) | copy-start | bytes 7077892
  111.6 1.4 %copy-start.1 = (f32[8,256]{1,0:T(8,128)S(1)}, f32[8,256]{1,0:T(8,128)}, u32[]{:S(2)}) copy-start(f32[8,256]{1,0:T(8,128)} %get-tuple-element.11) | copy-start | bytes 24580
